TPU v7x, 512 devices: a whole 4x4x16 slice. The times are simulated.
512 devices in a mesh: gy: 32 (over y_hi, z), gz: 16 (over y_lo, x, core).
Axes of the slice: x: 4, y: 4 (y_hi: 2, y_lo: 2; y = y_hi * 2 + y_lo), z: 16, core: 2. Of those that a mesh axis runs over, the one named last changes fastest.
Arguments:
- tokens: bfloat16 [2, 64, 32, 32, 1024], P(None, None, 'gy', 'gz'), may hold values from -64 to 64
- w_qkv: bfloat16 [1024, 3072], P('gy'), may hold values from -2 to 2
- w_out: bfloat16 [1024, 1024], P('gy'), may hold values from -0.1875 to 0.1875
- bias_x: float32 [16, 127], replicated, may hold values from -4 to 4
- bias_y: float32 [16, 63], replicated, may hold values from -4 to 4
- bias_z: float32 [16, 63], replicated, may hold values from -4 to 4
Outputs:
- mixed: bfloat16 [2, 64, 32, 32, 1024], P(None, None, 'gy', 'gz')
All inputs are finite; a program needn't handle non-finite values.
Results may differ from a plain program's by a relative error of at most 0.0083.
Values may be sent and summed in bfloat16 or wider, within the bound.
No kernel may reach another device: no remote copies, remote signals or barrier semaphores. Data moves between devices by JAX's collectives and lax.ppermute only.
A program may use at most 64 MiB of HBM per device.

v0:
```python
import jax
import jax.numpy as jnp
from jax import lax
from jax.sharding import Mesh
from jax.sharding import PartitionSpec as P

HEADS = 16
HEAD = 64
GY = ("gy_0", "gy_1")
einsum_forms = {
    1: ("bxyzhs,bwyzhs->byzhxw", "byzhxw,bwyzhs->bxyzhs"),
    2: ("bxyzhs,bxwzhs->bxzhyw", "bxzhyw,bxwzhs->bxyzhs"),
    3: ("bxyzhs,bxywhs->bxyhzw", "bxyhzw,bxywhs->bxyzhs"),
}


def laid_out(tiles, dim):
    tiles = jnp.moveaxis(tiles, 0, dim)
    shape = tiles.shape
    return tiles.reshape(*shape[:dim], shape[dim] * shape[dim + 1], *shape[dim + 2 :])


def stacked_from(shard, axes, sequence):
    tiles = shard[None]
    for k in sequence:
        tiles = lax.all_gather(tiles, axes[k], axis=0, tiled=True)
    held = [lax.axis_size(axes[k]) for k in reversed(sequence)]
    tiles = tiles.reshape(*held, *shard.shape)
    turned = sorted(range(len(sequence)), key=lambda place: sequence[len(sequence) - 1 - place])
    return tiles.transpose(*turned, *range(len(sequence), tiles.ndim)).reshape(-1, *shard.shape)


def gathered_by_axis(shard, axes, sequence, dim):
    return laid_out(stacked_from(shard, axes, sequence), dim)


def grouped_exchange(shard, axis, split_dim, concat_dim, work, item_dim, out_dim):

    def moved(group):
        return lax.all_to_all(group, axis, split_axis=split_dim, concat_axis=concat_dim, tiled=True)

    items = jax.tree.leaves(shard)[0].shape[item_dim]
    ends = [items * k // 2 for k in range(2 + 1)] if items % 2 == 0 else [0, items]
    groups = [
        jax.tree.map(lambda a: lax.slice_in_dim(a, low, high, axis=item_dim), shard)
        for low, high in zip(ends, ends[1:])
    ]
    arrived = [moved(group) for group in groups]
    made = [work(group) for group in arrived]
    return jax.tree.map(lambda *parts: jnp.concatenate(parts, axis=out_dim), *made)


def norm_rows(tokens):
    values = tokens.astype(jnp.float32)
    center = jnp.mean(values, axis=-1, keepdims=True)
    spread = jnp.mean((values - center) ** 2, axis=-1, keepdims=True)
    return ((values - center) * lax.rsqrt(spread + 1e-05)).astype(jnp.bfloat16)


def rel_bias(table):
    length = (table.shape[1] + 1) // 2
    offsets = (
        lax.broadcasted_iota(jnp.int32, (length, length), 0)
        - lax.broadcasted_iota(jnp.int32, (length, length), 1)
        + length
        - 1
    )
    lookup = (
        offsets[:, :, None] == lax.broadcasted_iota(jnp.int32, (1, 1, 2 * length - 1), 2)
    ).astype(jnp.float32)
    return jnp.einsum("hr,ijr->hij", table, lookup, precision=lax.Precision.HIGHEST)


def attend(qkv, table, axis):
    dims = qkv.shape
    features = dims[-1] // 3
    parts = qkv.reshape(dims[:-1] + (3, HEADS, HEAD))
    query = parts[..., 0, :, :]
    keys = parts[..., 1, :, :]
    values = parts[..., 2, :, :]
    score_form, mix_form = einsum_forms[axis]
    scores = jnp.einsum(score_form, query, keys, preferred_element_type=jnp.float32) * HEAD ** (
        -0.5
    ) + rel_bias(table)
    scores = scores - jnp.max(scores, axis=-1, keepdims=True)
    expo = jnp.exp(scores)
    weights = (expo / jnp.sum(expo, axis=-1, keepdims=True)).astype(jnp.bfloat16)
    mixed = jnp.einsum(mix_form, weights, values, preferred_element_type=jnp.float32)
    return mixed.reshape(dims[:-1] + (features,)).astype(jnp.bfloat16)


def return_y(result):
    return lax.all_to_all(result, GY, split_axis=2, concat_axis=1, tiled=True)


def return_z(result):
    return lax.all_to_all(result, "gz", split_axis=3, concat_axis=1, tiled=True)


def shards(tokens, w_qkv, w_out, bias_x, bias_y, bias_z):
    samples, depth, rows_y, rows_z, features = tokens.shape
    normed = norm_rows(tokens)
    gathered = gathered_by_axis(w_qkv, GY, (0, 1), 0)

    def project(inputs):
        product = jnp.dot(
            inputs.reshape(-1, features), gathered, preferred_element_type=jnp.float32
        )
        return product.astype(jnp.bfloat16).reshape(inputs.shape[:-1] + (3 * features,))

    def z_attention_inputs(lines):
        return return_z(attend(project(lines), bias_z, 3))

    along_x = attend(project(normed), bias_x, 1)
    along_y = return_y(
        attend(
            project(lax.all_to_all(normed, GY, split_axis=1, concat_axis=2, tiled=True)), bias_y, 2
        )
    )
    along_z = grouped_exchange(normed, "gz", 1, 3, z_attention_inputs, 0, 0)
    summed = along_x.astype(jnp.float32) + along_y.astype(jnp.float32) + along_z.astype(jnp.float32)
    summed = summed.astype(jnp.bfloat16).reshape(-1, features)
    residual = tokens.reshape(-1, features).astype(jnp.float32)
    result = residual + jnp.dot(
        summed, gathered_by_axis(w_out, GY, (0, 1), 0), preferred_element_type=jnp.float32
    )
    return result.astype(jnp.bfloat16).reshape(tokens.shape)


def solution(mesh):
    torus = Mesh(mesh.devices.reshape(2, 16, mesh.shape["gz"]), ("gy_0", "gy_1", "gz"))
    in_specs = (P(None, None, GY, "gz", None), P(GY, None), P(GY, None), P(), P(), P())
    out_specs = P(None, None, GY, "gz", None)
    return jax.shard_map(
        shards, mesh=torus, in_specs=in_specs, out_specs=out_specs, check_vma=False
    )
```

profile of v0, /device:TPU:1, one launch (start us, length us, event | category | flops | bytes accessed | tf_op | source)
XLA Modules:
  0.0 258.1 jit_solution(5049971114567313379)
XLA Ops:
  6.5 9.5 %all-gather = bf16[64,3072]{1,0:T(8,128)(2,1)} all-gather(bf16[32,3072]{1,0:T(8,128)(2,1)} %param.7), channel_id=2, replica_groups=mesh['gy_0'=2,'gy_1'=16,'gz'=16] {'gy_0'}, dimensions={0}, use_global_device_ids=true | all-gather | bytes 589824 | tf_op jit(solution)/shard_map/all_gather | solution.py:26
  16.1 1.6 convert_reduce_fusion
  17.7 1.9 multiply_reduce_fusion
  19.7 1.4 multiply_convert_fusion
  21.1 1.4 fusion.45
  22.5 15.3 %all_to_all.84 = bf16[1,64,1,2,1024]{4,3,2,0,1:T(2,128)(2,1)S(1)} all-to-all(bf16[1,64,1,2,1024]{4,3,2,0,1:T(2,128)(2,1)S(1)} %get-tuple-element.17), channel_id=1, replica_groups=mesh['gy_0'=2,'gy_1'=16,'gz'=16] {'gz'}, dimensions={1} | all-to-all | bytes 524288 | tf_op jit(solution)/shard_map/all_to_all | solution.py:40
  37.9 10.5 %all_to_all.85 = bf16[1,64,1,2,1024]{4,3,2,0,1:T(2,128)(2,1)S(1)} all-to-all(bf16[1,64,1,2,1024]{4,3,2,0,1:T(2,128)(2,1)S(1)} %get-tuple-element.18), channel_id=1, replica_groups=mesh['gy_0'=2,'gy_1'=16,'gz'=16] {'gz'}, dimensions={1} | all-to-all | bytes 524288 | tf_op jit(solution)/shard_map/all_to_all | solution.py:40
  48.3 15.8 %all-to-all-start = ((bf16[2,64,1,2,1024]{4,3,2,0,1:T(2,128)(2,1)}), bf16[2,64,1,2,1024]{4,3,2,0,1:T(2,128)(2,1)S(1)}, u32[]{:S(2)}, u32[]{:S(2)}) async-start(bf16[2,64,1,2,1024]{4,3,2,0,1:T(2,128)(2,1)} %multiply_convert_fusion), calls=%async_computation | async-start | bytes 1048576 | tf_op jit(solution)/shard_map/all_to_all | solution.py:117
  64.1 5.4 %all-gather.1 = bf16[64,1024]{1,0:T(8,128)(2,1)} all-gather(bf16[32,1024]{1,0:T(8,128)(2,1)S(1)} %copy-done.12), channel_id=3, replica_groups=mesh['gy_0'=2,'gy_1'=16,'gz'=16] {'gy_0'}, dimensions={0}, use_global_device_ids=true | all-gather | bytes 196608 | tf_op jit(solution)/shard_map/all_gather | solution.py:26
  69.6 1.2 convolution_bitcast_fusion
  71.0 1.2 convolution_bitcast_fusion.1
  73.6 28.8 %all-to-all-done = bf16[2,64,1,2,1024]{4,3,2,0,1:T(2,128)(2,1)S(1)} async-done(((bf16[2,64,1,2,1024]{4,3,2,0,1:T(2,128)(2,1)}), bf16[2,64,1,2,1024]{4,3,2,0,1:T(2,128)(2,1)S(1)}, u32[]{:S(2)}, u32[]{:S(2)}) %all-to-all-start) | async-done | bytes 524320 | tf_op jit(solution)/shard_map/all_to_all | solution.py:117
  103.0 24.8 %all-gather.5.cloned.1.call-done = bf16[32,32,3072]{2,1,0:T(8,128)(2,1)} async-done(((bf16[2,32,3072]{2,1,0:T(8,128)(2,1)}), bf16[32,32,3072]{2,1,0:T(8,128)(2,1)}) %all-gather.5.cloned.1.call-update) | async-done | bytes 6291472 | tf_op jit(solution)/shard_map/all_gather | solution.py:26
  127.9 3.2 %copy.142 = bf16[2,16,32,3072]{3,2,1,0:T(8,128)(2,1)S(1)} copy(bf16[2,16,32,3072]{3,2,0,1:T(8,128)(2,1)} %bitcast.195) | data formatting | bytes 12582912 | tf_op jit(solution)/shard_map/transpose | solution.py:30
  131.1 2.7 %copy-done.1 = bf16[2,16,32,3072]{3,2,1,0:T(8,128)(2,1)} copy-done((bf16[2,16,32,3072]{3,2,1,0:T(8,128)(2,1)}, bf16[2,16,32,3072]{3,2,1,0:T(8,128)(2,1)S(1)}, u32[]{:S(2)}) %copy-start.1) | copy-done | bytes 6291480
  135.8 1.3 fusion.43
  137.1 2.8 %fusion.48 = (f32[4,16,32]{2,1,0:T(8,128)S(1)}, f32[4,16,32,32]{2,3,1,0:T(8,128)}) fusion(bf16[1,4,1,32,1,16,64]{6,5,4,3,1,2,0:T(8,128)(2,1)} %get-tuple-element.13, bf16[1,4,1,32,1,16,64]{6,5,4,3,1,2,0:T(8,128)(2,1)} %get-tuple-element.12, f32[16,32,32]{1,2,0:T(8,128)S(1)} %copy.162), kind=kOutput, calls=%fused_computation.95 | convolution fusion | flops 8650783 | bytes 860160 | tf_op jit(solution)/shard_map/sub | solution.py:85
  140.0 1.6 fusion.20
  142.8 8.2 %all-to-all-start.3 = ((bf16[1,4,1,32,1024]{4,1,2,0,3:T(4,128)(2,1)}), bf16[1,4,1,32,1024]{4,1,2,0,3:T(4,128)(2,1)S(1)}, u32[]{:S(2)}, u32[]{:S(2)}) async-start(bf16[1,4,1,32,1024]{4,1,2,0,3:T(4,128)(2,1)} %reshape.299), calls=%async_computation.3 | async-start | bytes 524288 | tf_op jit(solution)/shard_map/all_to_all | solution.py:97
  151.0 3.8 %convolution_convert_fusion.2 = bf16[128,3072]{1,0:T(8,128)(2,1)S(1)} fusion(bf16[128,1024]{1,0:T(8,128)(2,1)S(1)} %reshape.283, bf16[1024,3072]{1,0:T(8,128)(2,1)} %bitcast.191), kind=kOutput, calls=%fused_computation.6 | convolution fusion | flops 805699584 | bytes 7340032 | tf_op jit(solution)/shard_map/dot_general | solution.py:106
  157.0 2.8 %fusion.47 = (f32[4,16,32]{2,1,0:T(8,128)S(1)}, f32[4,16,32,32]{2,3,1,0:T(8,128)}) fusion(bf16[1,4,1,32,1,16,64]{6,5,4,3,1,2,0:T(8,128)(2,1)} %get-tuple-element.16, bf16[1,4,1,32,1,16,64]{6,5,4,3,1,2,0:T(8,128)(2,1)S(1)} %get-tuple-element.15, f32[16,32,32]{1,2,0:T(8,128)} %copy-done.11), kind=kOutput, calls=%fused_computation.94 | convolution fusion | flops 8650783 | bytes 860160 | tf_op jit(solution)/shard_map/sub | solution.py:85
  159.8 1.6 fusion.21
  162.6 5.8 %convolution_convert_fusion = bf16[256,3072]{1,0:T(8,128)(2,1)} fusion(bf16[256,1024]{1,0:T(8,128)(2,1)S(1)} %reshape.278, bf16[1024,3072]{1,0:T(8,128)(2,1)} %bitcast.192), kind=kOutput, calls=%fused_computation.4 | convolution fusion | flops 1611399168 | bytes 8388608 | tf_op jit(solution)/shard_map/dot_general | solution.py:106
  168.4 3.6 %reshape_reshape.20 = bf16[2,2,32,2,3,16,64]{6,5,4,3,2,1,0:T(8,128)(2,1)S(1)} reshape(bf16[256,3072]{1,0:T(8,128)(2,1)} %convolution_convert_fusion) | data formatting | bytes 3145728 | tf_op jit(solution)/shard_map/reshape;reshape | solution.py:77
  172.1 2.0 fusion.42
  174.0 4.3 %fusion.46 = (f32[2,2,2,16,32]{4,3,2,1,0:T(8,128)S(1)}, f32[2,2,2,16,32,32]{4,5,3,2,1,0:T(8,128)}) fusion(f32[16,32,32]{1,2,0:T(8,128)} %copy.152, bf16[2,2,32,2,1,16,64]{6,5,4,3,2,1,0:T(8,128)(2,1)} %get-tuple-element.10, bf16[2,2,32,2,1,16,64]{6,5,4,3,2,1,0:T(8,128)(2,1)} %get-tuple-element.9), kind=kOutput, calls=%fused_computation.93 | convolution fusion | flops 17301536 | bytes 1654784 | tf_op jit(solution)/shard_map/sub | solution.py:85
  178.3 5.7 %all-to-all-start.5 = ((bf16[1,4,1,32,1024]{4,1,2,0,3:T(4,128)(2,1)}), bf16[1,4,1,32,1024]{4,1,2,0,3:T(4,128)(2,1)S(1)}, u32[]{:S(2)}, u32[]{:S(2)}) async-start(bf16[1,4,1,32,1024]{4,1,2,0,3:T(4,128)(2,1)} %reshape.300), calls=%async_computation.5 | async-start | bytes 524288 | tf_op jit(solution)/shard_map/all_to_all | solution.py:97
  184.0 2.3 fusion.13
  186.8 1.4 reshape.298
  188.1 3.1 %all-to-all-done.5 = bf16[1,4,1,32,1024]{4,1,2,0,3:T(4,128)(2,1)S(1)} async-done(((bf16[1,4,1,32,1024]{4,1,2,0,3:T(4,128)(2,1)}), bf16[1,4,1,32,1024]{4,1,2,0,3:T(4,128)(2,1)S(1)}, u32[]{:S(2)}, u32[]{:S(2)}) %all-to-all-start.5) | async-done | bytes 262176 | tf_op jit(solution)/shard_map/all_to_all | solution.py:97
  191.2 9.9 %all-to-all-start.1 = ((bf16[2,2,32,2,1024]{4,3,1,0,2:T(2,128)(2,1)}), bf16[2,2,32,2,1024]{4,3,1,0,2:T(2,128)(2,1)}, u32[]{:S(2)}, u32[]{:S(2)}) async-start(bf16[2,2,32,2,1024]{4,3,1,0,2:T(2,128)(2,1)} %reshape.298), calls=%async_computation.1 | async-start | bytes 1048576 | tf_op jit(solution)/shard_map/all_to_all | solution.py:93
  201.1 1.5 copy.141
  202.8 3.2 %fusion.19 = f32[16,64,64]{2,0,1:T(8,128)S(1)} fusion(s32[64,64]{1,0:T(8,128)S(1)} %subtract_add_fusion, f32[16,127]{1,0:T(8,128)S(1)} %copy-done), kind=kOutput, calls=%fused_computation.38 | convolution fusion | flops 100397056 | bytes 286656 | tf_op jit(solution)/shard_map/hr,ijr->hij/dot_general | solution.py:71
  207.7 1.7 reshape.289
  209.4 3.2 %copy.178 = bf16[2,16,32,1024]{3,2,1,0:T(8,128)(2,1)} copy(bf16[2,16,32,1024]{3,2,0,1:T(8,128)(2,1)} %bitcast.196) | data formatting | bytes 4194304 | tf_op jit(solution)/shard_map/transpose | solution.py:30
  212.7 5.7 %convolution_convert_fusion.1 = bf16[256,3072]{1,0:T(8,128)(2,1)} fusion(bf16[256,1024]{1,0:T(8,128)(2,1)S(1)} %reshape.273, bf16[1024,3072]{1,0:T(8,128)(2,1)} %bitcast.193), kind=kOutput, calls=%fused_computation.5 | convolution fusion | flops 1611399168 | bytes 8388608 | tf_op jit(solution)/shard_map/dot_general | solution.py:106
  218.4 3.6 %reshape_reshape.19 = bf16[2,64,1,2,3,16,64]{6,5,4,3,1,0,2:T(8,128)(2,1)S(1)} reshape(bf16[256,3072]{1,0:T(8,128)(2,1)} %convolution_convert_fusion.1) | data formatting | bytes 3145728 | tf_op jit(solution)/shard_map/reshape;reshape | solution.py:77
  222.1 2.0 fusion.41
  224.1 3.1 %copy.190 = bf16[2,64,1,2,1,16,64]{1,6,5,3,0,4,2:T(8,128)(2,1)} copy(bf16[2,64,1,2,1,16,64]{6,5,4,3,1,0,2:T(8,128)(2,1)} %get-tuple-element.5) | data formatting | bytes 1048576
  227.1 3.7 %fusion.49 = (f32[2,2,16,64]{3,2,1,0:T(8,128)S(1)}, f32[2,2,16,64,64]{3,4,2,1,0:T(8,128)}) fusion(f32[16,64,64]{1,2,0:T(8,128)} %copy.146, bf16[2,64,1,2,1,16,64]{6,5,4,3,1,0,2:T(8,128)(2,1)S(1)} %copy-done.9, bf16[2,64,1,2,1,16,64]{6,5,4,3,1,0,2:T(8,128)(2,1)S(1)} %copy-done.10), kind=kOutput, calls=%fused_computation.96 | convolution fusion | flops 34603072 | bytes 2375680 | tf_op jit(solution)/shard_map/sub | solution.py:85
  231.4 1.4 copy.175
  233.4 1.4 copy.176
  234.8 1.6 convert_bitcast_fusion.1
  237.6 2.2 copy.157
  239.9 4.0 %fusion.6 = bf16[2,64,1,2,16,64]{1,5,4,3,0,2:T(8,128)(2,1)} fusion(f32[2,64,1,2,16,64]{1,5,4,3,0,2:T(8,128)} %copy.157, f32[2,2,16,64,64]{3,4,2,1,0:T(8,128)} %get-tuple-element.26, bf16[1,64,1,2,16,64]{1,5,4,3,0,2:T(8,128)(2,1)} %copy.176, bf16[1,64,1,2,16,64]{1,5,4,3,0,2:T(8,128)(2,1)} %copy.175, bf16[2,64,1,2,1,16,64]{1,6,5,3,0,4,2:T(8,128)(2,1)S(1)} %copy-done.5, ...), kind=kOutput, calls=%fused_computation.11 | convolution fusion | flops 35913728 | bytes 3686400 | tf_op jit(solution)/shard_map/byzhxw,bwyzhs->bxyzhs/dot_general | solution.py:88
  243.9 2.7 %copy.177 = bf16[2,64,1,2,16,64]{5,4,3,1,0,2:T(8,128)(2,1)S(1)} copy(bf16[2,64,1,2,16,64]{1,5,4,3,0,2:T(8,128)(2,1)} %fusion.6) | data formatting | bytes 1048576 | tf_op jit(solution)/shard_map/convert_element_type | solution.py:122
  246.6 1.5 convert_element_type.194
  248.1 2.1 fusion.18
  (68 shorter events, 14.7 us)
Async XLA Ops:
  6.5 196.2 %copy-start = (f32[16,127]{1,0:T(8,128)S(1)}, f32[16,127]{1,0:T(8,128)}, u32[]{:S(2)}) copy-start(f32[16,127]{1,0:T(8,128)} %param.9) | copy-start | bytes 24388
  6.5 13.1 %copy-start.2 = (bf16[2,64,1,2,1024]{4,3,2,1,0:T(2,128)(2,1)S(1)}, bf16[2,64,1,2,1024]{4,3,2,1,0:T(2,128)(2,1)}, u32[]{:S(2)}) copy-start(bf16[2,64,1,2,1024]{4,3,2,1,0:T(2,128)(2,1)} %param.6) | copy-start | bytes 1572868
  6.5 121.3 %all-gather.5.cloned.1.call-start = ((), (), s32[]{:S(2)}) async-start(), calls=%async_computation.6 | async-start | bytes 6684672 | tf_op jit(solution)/shard_map/all_gather | solution.py:26
  19.7 44.5 %copy-start.12 = (bf16[32,1024]{1,0:T(8,128)(2,1)S(1)}, bf16[32,1024]{1,0:T(8,128)(2,1)}, u32[]{:S(2)}) copy-start(bf16[32,1024]{1,0:T(8,128)(2,1)} %param.8) | copy-start | bytes 196612
  19.7 49.9 %copy-start.13 = (f32[16,63]{1,0:T(8,128)S(1)}, f32[16,63]{1,0:T(8,128)}, u32[]{:S(2)}) copy-start(f32[16,63]{1,0:T(8,128)} %param.11) | copy-start | bytes 12100
  21.1 49.8 %copy-start.14 = (f32[16,63]{1,0:T(8,128)S(1)}, f32[16,63]{1,0:T(8,128)}, u32[]{:S(2)}) copy-start(f32[16,63]{1,0:T(8,128)} %param.10) | copy-start | bytes 12100
  48.3 54.2 %all-to-all-start = ((bf16[2,64,1,2,1024]{4,3,2,0,1:T(2,128)(2,1)}), bf16[2,64,1,2,1024]{4,3,2,0,1:T(2,128)(2,1)S(1)}, u32[]{:S(2)}, u32[]{:S(2)}) async-start(bf16[2,64,1,2,1024]{4,3,2,0,1:T(2,128)(2,1)} %multiply_convert_fusion), calls=%async_computation | async-start | bytes 1048576 | tf_op jit(solution)/shard_map/all_to_all | solution.py:117
  64.1 145.3 %all-gather.7.cloned.1.call-start = ((), (), s32[]{:S(2)}) async-start(), calls=%async_computation.7 | async-start | bytes 2228224 | tf_op jit(solution)/shard_map/all_gather | solution.py:26
  71.0 66.1 %copy-start.11 = (f32[16,32,32]{1,2,0:T(8,128)}, f32[16,32,32]{1,2,0:T(8,128)S(1)}, u32[]{:S(2)}) copy-start(f32[16,32,32]{1,2,0:T(8,128)S(1)} %copy.162) | copy-start | bytes 196612
  131.1 2.7 %copy-start.1 = (bf16[2,16,32,3072]{3,2,1,0:T(8,128)(2,1)}, bf16[2,16,32,3072]{3,2,1,0:T(8,128)(2,1)S(1)}, u32[]{:S(2)}) copy-start(bf16[2,16,32,3072]{3,2,1,0:T(8,128)(2,1)S(1)} %copy.142) | copy-start | bytes 18874372
  142.8 35.6 %all-to-all-start.3 = ((bf16[1,4,1,32,1024]{4,1,2,0,3:T(4,128)(2,1)}), bf16[1,4,1,32,1024]{4,1,2,0,3:T(4,128)(2,1)S(1)}, u32[]{:S(2)}, u32[]{:S(2)}) async-start(bf16[1,4,1,32,1024]{4,1,2,0,3:T(4,128)(2,1)} %reshape.299), calls=%async_computation.3 | async-start | bytes 524288 | tf_op jit(solution)/shard_map/all_to_all | solution.py:97
  174.0 10.0 %copy-start.8 = (bf16[2,2,32,2,1,16,64]{6,5,4,3,2,1,0:T(8,128)(2,1)S(1)}, bf16[2,2,32,2,1,16,64]{6,5,4,3,2,1,0:T(8,128)(2,1)}, u32[]{:S(2)}) copy-start(bf16[2,2,32,2,1,16,64]{6,5,4,3,2,1,0:T(8,128)(2,1)} %get-tuple-element.8) | copy-start | bytes 1572868
  178.3 12.9 %all-to-all-start.5 = ((bf16[1,4,1,32,1024]{4,1,2,0,3:T(4,128)(2,1)}), bf16[1,4,1,32,1024]{4,1,2,0,3:T(4,128)(2,1)S(1)}, u32[]{:S(2)}, u32[]{:S(2)}) async-start(bf16[1,4,1,32,1024]{4,1,2,0,3:T(4,128)(2,1)} %reshape.300), calls=%async_computation.5 | async-start | bytes 524288 | tf_op jit(solution)/shard_map/all_to_all | solution.py:97
  191.2 15.8 %copy-start.6 = (bf16[1,4,1,32,1024]{4,1,2,0,3:T(4,128)(2,1)}, bf16[1,4,1,32,1024]{4,1,2,0,3:T(4,128)(2,1)S(1)}, u32[]{:S(2)}) copy-start(bf16[1,4,1,32,1024]{4,1,2,0,3:T(4,128)(2,1)S(1)} %all-to-all-done.5) | copy-start | bytes 786436
  191.2 43.6 %all-to-all-start.1 = ((bf16[2,2,32,2,1024]{4,3,1,0,2:T(2,128)(2,1)}), bf16[2,2,32,2,1024]{4,3,1,0,2:T(2,128)(2,1)}, u32[]{:S(2)}, u32[]{:S(2)}) async-start(bf16[2,2,32,2,1024]{4,3,1,0,2:T(2,128)(2,1)} %reshape.298), calls=%async_computation.1 | async-start | bytes 1048576 | tf_op jit(solution)/shard_map/all_to_all | solution.py:93
  201.1 6.0 %copy-start.3 = (bf16[2,64,1,2,1024]{4,3,2,1,0:T(2,128)(2,1)S(1)}, bf16[2,64,1,2,1024]{4,3,2,1,0:T(2,128)(2,1)}, u32[]{:S(2)}) copy-start(bf16[2,64,1,2,1024]{4,3,2,1,0:T(2,128)(2,1)} %param.6) | copy-start | bytes 1572868
  224.0 3.1 %copy-start.9 = (bf16[2,64,1,2,1,16,64]{6,5,4,3,1,0,2:T(8,128)(2,1)S(1)}, bf16[2,64,1,2,1,16,64]{6,5,4,3,1,0,2:T(8,128)(2,1)}, u32[]{:S(2)}) copy-start(bf16[2,64,1,2,1,16,64]{6,5,4,3,1,0,2:T(8,128)(2,1)} %get-tuple-element.6) | copy-start | bytes 1572868
  224.1 3.1 %copy-start.10 = (bf16[2,64,1,2,1,16,64]{6,5,4,3,1,0,2:T(8,128)(2,1)S(1)}, bf16[2,64,1,2,1,16,64]{6,5,4,3,1,0,2:T(8,128)(2,1)}, u32[]{:S(2)}) copy-start(bf16[2,64,1,2,1,16,64]{6,5,4,3,1,0,2:T(8,128)(2,1)} %get-tuple-element.7) | copy-start | bytes 1572868
  230.8 2.0 copy-start.7
  237.6 2.3 copy-start.5
  243.9 4.3 %copy-start.4 = (bf16[2,16,32,1024]{3,2,1,0:T(8,128)(2,1)S(1)}, bf16[2,16,32,1024]{3,2,1,0:T(8,128)(2,1)}, u32[]{:S(2)}) copy-start(bf16[2,16,32,1024]{3,2,1,0:T(8,128)(2,1)} %copy.178) | copy-start | bytes 6291460
Sparse Core Ops, SparseCore 0:
  16.2 111.6 all-gather.4
  129.9 63.7 all-gather.6
where the time goes:
time: 259 us; the launch traced here: 258 us
  waiting for transfers between devices  56.7 us (22%)
  local copies, waits for them, and re-layouts  53 us (20%)
  matrix products  47.2 us (18%)
  blocking collectives  40.7 us (16%)
  starting transfers between devices  39.6 us (15%)
  between operations  13.8 us (5%)
  other arithmetic  7.16 us (3%)
    all_to_all x1, waiting for transfers between devices, shards(): lax.all_to_all(normed, GY, split_axis=1, concat_axis=2, tiled=True)  28.8 us
    all_to_all x2, blocking collectives, moved(): lax.all_to_all(group, axis, split_axis=split_dim, concat_axis=concat_dim,...  25.8 us
    all_gather x2, waiting for transfers between devices, stacked_from(): tiles = lax.all_gather(tiles, axes[k], axis=0, tiled=True)  24.8 us
    dot_general x4, matrix products, project(): jnp.dot(inputs.reshape(-1, features), gathered, preferred_element_type=jn...  16.4 us
    all_to_all x1, starting transfers between devices, shards(): lax.all_to_all(normed, GY, split_axis=1, concat_axis=2, tiled=True)  15.8 us
    all_gather x2, blocking collectives, stacked_from(): tiles = lax.all_gather(tiles, axes[k], axis=0, tiled=True)  14.9 us
    all_to_all x2, starting transfers between devices, return_z(): return lax.all_to_all(result, 'gz', split_axis=3, concat_axis=1, tiled=True)  13.9 us
    sub x4, matrix products, attend(): scores = scores - jnp.max(scores, axis=-1, keepdims=True)  13.6 us
  transfers between devices with their start and end apart: 6, of which 3 were waited for; matrix products, arithmetic and copies ran while one was open for 34% of the time, Pallas kernels for 0%

commit v1 on v0

--- a/solution.py
+++ b/solution.py
@@ -23,7 +23,16 @@
 def stacked_from(shard, axes, sequence):
     tiles = shard[None]
     for k in sequence:
-        tiles = lax.all_gather(tiles, axes[k], axis=0, tiled=True)
+        z_in = axes[k]
+        tiles = jnp.concatenate(
+            lax.all_to_all(
+                jnp.stack([tiles] * lax.axis_size(z_in), axis=0),
+                axis_name=z_in,
+                split_axis=0,
+                concat_axis=0,
+            ),
+            axis=0,
+        )
     held = [lax.axis_size(axes[k]) for k in reversed(sequence)]
     tiles = tiles.reshape(*held, *shard.shape)
     turned = sorted(range(len(sequence)), key=lambda place: sequence[len(sequence) - 1 - place])

time: 259 us -> 562 us (2.17)
  blocking collectives: 40.7 us -> 347 us
  between operations: 13.8 us -> 0.44 us
    all_to_all x0 -> x2, blocking collectives: none -> 320 us  [the longest x1 275 us: stacked_from(): lax.all_to_all(jnp.stack([tiles] * lax.axis_size(z_in), axis=0), axis_nam...]
    all_to_all x1 -> x3, waiting for transfers between devices: 28.8 us -> 55.6 us  [stacked_from(): lax.all_to_all(jnp.stack([tiles] * lax.axis_size(z_in), axis=0), axis_nam...]
    all_gather x2 -> x0, waiting for transfers between devices: 24.8 us -> none  [stacked_from(): tiles = lax.all_gather(tiles, axes[k], axis=0, tiled=True)]
    all_gather x2 -> x0, blocking collectives: 14.9 us -> none  [stacked_from(): tiles = lax.all_gather(tiles, axes[k], axis=0, tiled=True)]
    transpose x2 -> x0, local copies, waits for them, and re-layouts: 6.46 us -> none  [stacked_from(): tiles.transpose(*turned, *range(len(sequence), tiles.ndim))]
    all_to_all x0 -> x2, local copies, waits for them, and re-layouts: none -> 6.45 us  [stacked_from(): lax.all_to_all(jnp.stack([tiles] * lax.axis_size(z_in), axis=0), axis_nam...]
    all_to_all x1 -> x3, starting transfers between devices: 15.8 us -> 21.6 us  [stacked_from(): lax.all_to_all(jnp.stack([tiles] * lax.axis_size(z_in), axis=0), axis_nam...]
  transfers between devices with their start and end apart: 6 -> 6, of which waited for: 3 -> 4; matrix products, arithmetic and copies ran while one was open for 34% -> 15% of each run, Pallas kernels for 0% -> 0%
where the time goes in v1:
time: 562 us; the launch traced here: 560 us
  blocking collectives  347 us (62%)
  waiting for transfers between devices  61.7 us (11%)
  local copies, waits for them, and re-layouts  53.2 us (9%)
  matrix products  46.8 us (8%)
  starting transfers between devices  42.2 us (8%)
  other arithmetic  8.72 us (2%)
    all_to_all x1, blocking collectives, stacked_from(): lax.all_to_all(jnp.stack([tiles] * lax.axis_size(z_in), axis=0), axis_nam...  275 us
    all_to_all x3, waiting for transfers between devices, stacked_from(): lax.all_to_all(jnp.stack([tiles] * lax.axis_size(z_in), axis=0), axis_nam...  55.6 us
    all_to_all x1, blocking collectives, shards(): lax.all_to_all(normed, GY, split_axis=1, concat_axis=2, tiled=True)  45.2 us
    all_to_all x2, blocking collectives, moved(): lax.all_to_all(group, axis, split_axis=split_dim, concat_axis=concat_dim,...  27 us
    all_to_all x3, starting transfers between devices, stacked_from(): lax.all_to_all(jnp.stack([tiles] * lax.axis_size(z_in), axis=0), axis_nam...  21.6 us
    dot_general x4, matrix products, project(): jnp.dot(inputs.reshape(-1, features), gathered, preferred_element_type=jn...  16.3 us
    sub x4, matrix products, attend(): scores = scores - jnp.max(scores, axis=-1, keepdims=True)  13.3 us
    all_to_all x2, starting transfers between devices, return_z(): return lax.all_to_all(result, 'gz', split_axis=3, concat_axis=1, tiled=True)  12.9 us
  transfers between devices with their start and end apart: 6, of which 4 were waited for; matrix products, arithmetic and copies ran while one was open for 15% of the time, Pallas kernels for 0%

profile of v1, /device:TPU:1, one launch (start us, length us, event | category | flops | bytes accessed | tf_op | source)
XLA Modules:
  0.0 560.4 jit_solution(12601702568449260412)
XLA Ops:
  0.0 1.6 pad_maximum_fusion.1
  1.6 5.0 all-to-all-start.8
  6.6 1.6 convert_reduce_fusion
  8.2 1.9 multiply_reduce_fusion
  11.7 4.2 all-to-all-start
  16.3 5.9 %all-to-all-done = bf16[2,1,32,3072]{3,2,1,0:T(8,128)(2,1)S(1)} async-done(((bf16[2,1,32,3072]{3,2,1,0:T(8,128)(2,1)}), bf16[2,1,32,3072]{3,2,1,0:T(8,128)(2,1)S(1)}, u32[]{:S(2)}, u32[]{:S(2)}) %all-to-all-start) | async-done | bytes 393248 | tf_op jit(solution)/shard_map/all_to_all | solution.py:28
  22.1 16.6 %all_to_all.104 = bf16[1,64,1,2,1024]{4,3,2,0,1:T(2,128)(2,1)S(1)} all-to-all(bf16[1,64,1,2,1024]{4,3,2,0,1:T(2,128)(2,1)S(1)} %get-tuple-element.17), channel_id=1, replica_groups=mesh['gy_0'=2,'gy_1'=16,'gz'=16] {'gz'}, dimensions={1} | all-to-all | bytes 524288 | tf_op jit(solution)/shard_map/all_to_all | solution.py:49
  38.7 10.5 %all_to_all.105 = bf16[1,64,1,2,1024]{4,3,2,0,1:T(2,128)(2,1)S(1)} all-to-all(bf16[1,64,1,2,1024]{4,3,2,0,1:T(2,128)(2,1)S(1)} %get-tuple-element.18), channel_id=1, replica_groups=mesh['gy_0'=2,'gy_1'=16,'gz'=16] {'gz'}, dimensions={1} | all-to-all | bytes 524288 | tf_op jit(solution)/shard_map/all_to_all | solution.py:49
  49.2 45.2 %all_to_all.106 = bf16[2,64,1,2,1024]{4,3,2,0,1:T(2,128)(2,1)S(1)} all-to-all(bf16[2,64,1,2,1024]{4,3,2,0,1:T(2,128)(2,1)S(1)} %multiply_convert_fusion), channel_id=1, replica_groups=mesh['gy_0'=2,'gy_1'=16,'gz'=16] {'gy_0','gy_1'}, dimensions={1} | all-to-all | bytes 1048576 | tf_op jit(solution)/shard_map/all_to_all | solution.py:126
  95.1 275.2 %all_to_all.107 = bf16[16,2,32,3072]{3,2,1,0:T(8,128)(2,1)} all-to-all(bf16[16,2,32,3072]{3,2,1,0:T(8,128)(2,1)S(1)} %stack.13), channel_id=1, replica_groups=mesh['gy_0'=2,'gy_1'=16,'gz'=16] {'gy_1'}, dimensions={0} | all-to-all | bytes 12582912 | tf_op jit(solution)/shard_map/all_to_all | solution.py:28
  370.3 1.6 stack.15
  372.0 12.3 %all-to-all-start.9 = ((bf16[16,2,32,1024]{3,2,1,0:T(8,128)(2,1)}), bf16[16,2,32,1024]{3,2,1,0:T(8,128)(2,1)}, u32[]{:S(2)}, u32[]{:S(2)}) async-start(bf16[16,2,32,1024]{3,2,1,0:T(8,128)(2,1)} %stack.15), calls=%async_computation.9 | async-start | bytes 4194304 | tf_op jit(solution)/shard_map/all_to_all | solution.py:28
  388.9 3.2 copy.105
  392.2 2.6 copy-done.1
  396.8 1.3 fusion.43
  398.2 2.8 fusion.48
  400.9 1.6 fusion.20
  403.8 3.8 convolution_convert_fusion.2
  409.7 2.6 fusion.47
  412.4 1.6 fusion.21
  415.1 5.8 %convolution_convert_fusion = bf16[256,3072]{1,0:T(8,128)(2,1)} fusion(bf16[256,1024]{1,0:T(8,128)(2,1)S(1)} %reshape.275, bf16[1024,3072]{1,0:T(8,128)(2,1)} %bitcast.192), kind=kOutput, calls=%fused_computation.4 | convolution fusion | flops 1611399168 | bytes 8388608 | tf_op jit(solution)/shard_map/dot_general | solution.py:115
  420.9 3.6 reshape_reshape.20
  424.5 2.0 fusion.42
  426.5 49.7 %all-to-all-done.9 = bf16[16,2,32,1024]{3,2,1,0:T(8,128)(2,1)} async-done(((bf16[16,2,32,1024]{3,2,1,0:T(8,128)(2,1)}), bf16[16,2,32,1024]{3,2,1,0:T(8,128)(2,1)}, u32[]{:S(2)}, u32[]{:S(2)}) %all-to-all-start.9) | async-done | bytes 2097184 | tf_op jit(solution)/shard_map/all_to_all | solution.py:28
  476.2 8.8 %all-to-all-start.5 = ((bf16[1,4,1,32,1024]{4,1,2,0,3:T(4,128)(2,1)}), bf16[1,4,1,32,1024]{4,1,2,0,3:T(4,128)(2,1)S(1)}, u32[]{:S(2)}, u32[]{:S(2)}) async-start(bf16[1,4,1,32,1024]{4,1,2,0,3:T(4,128)(2,1)} %reshape.293), calls=%async_computation.5 | async-start | bytes 524288 | tf_op jit(solution)/shard_map/all_to_all | solution.py:106
  485.0 4.3 fusion.46
  489.3 3.0 all-to-all-done.5
  492.2 4.1 all-to-all-start.7
  496.4 2.3 fusion.13
  499.1 1.4 reshape.292
  500.5 3.1 all-to-all-done.7
  503.6 7.7 %all-to-all-start.3 = ((bf16[2,2,32,2,1024]{4,3,1,0,2:T(2,128)(2,1)}), bf16[2,2,32,2,1024]{4,3,1,0,2:T(2,128)(2,1)}, u32[]{:S(2)}, u32[]{:S(2)}) async-start(bf16[2,2,32,2,1024]{4,3,1,0,2:T(2,128)(2,1)} %reshape.292), calls=%async_computation.3 | async-start | bytes 1048576 | tf_op jit(solution)/shard_map/all_to_all | solution.py:102
  511.9 3.2 fusion.19
  516.8 1.7 reshape.285
  518.6 3.2 copy.141
  521.8 5.8 %convolution_convert_fusion.1 = bf16[256,3072]{1,0:T(8,128)(2,1)} fusion(bf16[256,1024]{1,0:T(8,128)(2,1)S(1)} %reshape.271, bf16[1024,3072]{1,0:T(8,128)(2,1)} %bitcast.193), kind=kOutput, calls=%fused_computation.5 | convolution fusion | flops 1611399168 | bytes 8388608 | tf_op jit(solution)/shard_map/dot_general | solution.py:115
  527.5 3.6 reshape_reshape.19
  531.2 2.0 fusion.41
  533.2 3.1 copy.153
  536.2 3.7 fusion.49
  540.5 1.4 copy.138
  542.5 1.4 copy.139
  543.9 1.6 convert_bitcast_fusion.1
  546.7 2.2 copy.120
  549.0 4.0 fusion.6
  553.0 2.7 copy.140
  555.7 1.5 convert_element_type.194
  557.2 2.1 fusion.18
  (72 shorter events, 19.9 us)
Async XLA Ops:
  0.0 511.9 %copy-start = (f32[16,127]{1,0:T(8,128)S(1)}, f32[16,127]{1,0:T(8,128)}, u32[]{:S(2)}) copy-start(f32[16,127]{1,0:T(8,128)} %param.9) | copy-start | bytes 24388
  0.0 11.0 %copy-start.2 = (bf16[2,64,1,2,1024]{4,3,2,1,0:T(2,128)(2,1)S(1)}, bf16[2,64,1,2,1024]{4,3,2,1,0:T(2,128)(2,1)}, u32[]{:S(2)}) copy-start(bf16[2,64,1,2,1024]{4,3,2,1,0:T(2,128)(2,1)} %param.6) | copy-start | bytes 1572868
  0.0 10.2 %copy-start.13 = (bf16[32,3072]{1,0:T(8,128)(2,1)S(1)}, bf16[32,3072]{1,0:T(8,128)(2,1)}, u32[]{:S(2)}) copy-start(bf16[32,3072]{1,0:T(8,128)(2,1)} %param.7) | copy-start | bytes 589828
  1.6 10.0 %all-to-all-start.8 = ((bf16[2,1,32,1024]{3,2,1,0:T(8,128)(2,1)}), bf16[2,1,32,1024]{3,2,1,0:T(8,128)(2,1)S(1)}, u32[]{:S(2)}, u32[]{:S(2)}) async-start(bf16[2,1,32,1024]{3,2,1,0:T(8,128)(2,1)} %pad_maximum_fusion.1), calls=%async_computation.8 | async-start | bytes 262144 | tf_op jit(solution)/shard_map/all_to_all | solution.py:28
  11.6 83.5 %copy-start.5 = (bf16[2,64,1,2,1024]{4,3,2,0,1:T(2,128)(2,1)}, bf16[2,64,1,2,1024]{4,3,2,0,1:T(2,128)(2,1)S(1)}, u32[]{:S(2)}) copy-start(bf16[2,64,1,2,1024]{4,3,2,0,1:T(2,128)(2,1)S(1)} %multiply_convert_fusion) | copy-start | bytes 1572868
  11.7 10.5 %all-to-all-start = ((bf16[2,1,32,3072]{3,2,1,0:T(8,128)(2,1)}), bf16[2,1,32,3072]{3,2,1,0:T(8,128)(2,1)S(1)}, u32[]{:S(2)}, u32[]{:S(2)}) async-start(bf16[2,1,32,3072]{3,2,1,0:T(8,128)(2,1)} %pad_maximum_fusion), calls=%async_computation | async-start | bytes 786432 | tf_op jit(solution)/shard_map/all_to_all | solution.py:28
  371.9 12.4 %copy-start.14 = (f32[16,63]{1,0:T(8,128)S(1)}, f32[16,63]{1,0:T(8,128)}, u32[]{:S(2)}) copy-start(f32[16,63]{1,0:T(8,128)} %param.11) | copy-start | bytes 12100
  371.9 13.7 %copy-start.15 = (f32[16,63]{1,0:T(8,128)S(1)}, f32[16,63]{1,0:T(8,128)}, u32[]{:S(2)}) copy-start(f32[16,63]{1,0:T(8,128)} %param.10) | copy-start | bytes 12100
  372.0 104.2 %all-to-all-start.9 = ((bf16[16,2,32,1024]{3,2,1,0:T(8,128)(2,1)}), bf16[16,2,32,1024]{3,2,1,0:T(8,128)(2,1)}, u32[]{:S(2)}, u32[]{:S(2)}) async-start(bf16[16,2,32,1024]{3,2,1,0:T(8,128)(2,1)} %stack.15), calls=%async_computation.9 | async-start | bytes 4194304 | tf_op jit(solution)/shard_map/all_to_all | solution.py:28
  392.2 2.7 copy-start.1
  476.2 16.0 %all-to-all-start.5 = ((bf16[1,4,1,32,1024]{4,1,2,0,3:T(4,128)(2,1)}), bf16[1,4,1,32,1024]{4,1,2,0,3:T(4,128)(2,1)S(1)}, u32[]{:S(2)}, u32[]{:S(2)}) async-start(bf16[1,4,1,32,1024]{4,1,2,0,3:T(4,128)(2,1)} %reshape.293), calls=%async_computation.5 | async-start | bytes 524288 | tf_op jit(solution)/shard_map/all_to_all | solution.py:106
  485.0 11.4 %copy-start.10 = (bf16[2,2,32,2,1,16,64]{6,5,4,3,2,1,0:T(8,128)(2,1)S(1)}, bf16[2,2,32,2,1,16,64]{6,5,4,3,2,1,0:T(8,128)(2,1)}, u32[]{:S(2)}) copy-start(bf16[2,2,32,2,1,16,64]{6,5,4,3,2,1,0:T(8,128)(2,1)} %get-tuple-element.8) | copy-start | bytes 1572868
  492.2 11.4 %all-to-all-start.7 = ((bf16[1,4,1,32,1024]{4,1,2,0,3:T(4,128)(2,1)}), bf16[1,4,1,32,1024]{4,1,2,0,3:T(4,128)(2,1)S(1)}, u32[]{:S(2)}, u32[]{:S(2)}) async-start(bf16[1,4,1,32,1024]{4,1,2,0,3:T(4,128)(2,1)} %reshape.294), calls=%async_computation.7 | async-start | bytes 524288 | tf_op jit(solution)/shard_map/all_to_all | solution.py:106
  498.7 12.6 %copy-start.6 = (bf16[2,64,1,2,1024]{4,3,2,0,1:T(2,128)(2,1)S(1)}, bf16[2,64,1,2,1024]{4,3,2,0,1:T(2,128)(2,1)}, u32[]{:S(2)}) copy-start(bf16[2,64,1,2,1024]{4,3,2,0,1:T(2,128)(2,1)} %copy-done.5) | copy-start | bytes 1572868
  503.6 12.6 %copy-start.8 = (bf16[1,4,1,32,1024]{4,1,2,0,3:T(4,128)(2,1)}, bf16[1,4,1,32,1024]{4,1,2,0,3:T(4,128)(2,1)S(1)}, u32[]{:S(2)}) copy-start(bf16[1,4,1,32,1024]{4,1,2,0,3:T(4,128)(2,1)S(1)} %all-to-all-done.7) | copy-start | bytes 786436
  503.6 40.3 %all-to-all-start.3 = ((bf16[2,2,32,2,1024]{4,3,1,0,2:T(2,128)(2,1)}), bf16[2,2,32,2,1024]{4,3,1,0,2:T(2,128)(2,1)}, u32[]{:S(2)}, u32[]{:S(2)}) async-start(bf16[2,2,32,2,1024]{4,3,1,0,2:T(2,128)(2,1)} %reshape.292), calls=%async_computation.3 | async-start | bytes 1048576 | tf_op jit(solution)/shard_map/all_to_all | solution.py:102
  511.3 4.9 copy-start.3
  533.2 3.1 copy-start.11
  533.2 3.1 copy-start.12
  539.9 2.0 copy-start.9
  546.7 2.3 copy-start.7
  553.0 4.3 copy-start.4
